TPU v7x, 256 devices: a whole 4x4x8 slice. The times are simulated.
256 devices in a mesh: dx: 16 (over z_hi, x, core), dy: 16 (over z_lo, y).
Axes of the slice: x: 4, y: 4, z: 8 (z_hi: 2, z_lo: 4; z = z_hi * 4 + z_lo), core: 2. Of those that a mesh axis runs over, the one named last changes fastest.
Arguments:
- features: bfloat16 [16, 16, 384, 128], P('dx', 'dy'), may hold values from -6 to 6
- positions: bfloat16 [16, 16, 3, 384], P('dx', 'dy'), may hold values from 0 to 1
- atom_count: int32 [16, 16], P('dx', 'dy'), may hold values from 192 to 384, as said below
- ghost_index: int32 [16, 16, 256], P('dx', 'dy'), may hold values from 0 to 383, as said below
- neighbour_list: int32 [16, 16, 384, 32], P('dx', 'dy'), may hold values from 0 to 2687, as said below
- cell_index: int32 [16, 16, 384], P('dx', 'dy'), may hold values from 0 to 65535
- w_self: bfloat16 [128, 128], replicated, may hold values from -0.5 to 0.5
- w_pair: bfloat16 [128, 256], replicated, may hold values from -0.5 to 0.5
- w_radial: float32 [8, 128], replicated, may hold values from -2 to 2
- w_expand: bfloat16 [128, 1024], replicated, may hold values from -0.5 to 0.5
- w_contract: bfloat16 [1024, 128], replicated, may hold values from -0.1875 to 0.1875
- w_final: bfloat16 [128, 128], replicated, may hold values from -0.5 to 0.5
- w_charge: bfloat16 [128], replicated, may hold values from -0.5 to 0.5
Outputs:
- forces: float32 [16, 16, 3, 384], P('dx', 'dy')
Inputs may be any that keep to these rules, and one draw needn't show every extreme that they name: `atom_count`: each domain holds at least half of 384 live atoms in its first slots, and some domain is full. `ghost_index`: each entry is a live slot of the same domain. `neighbour_list`: each entry is a live slot of the domain itself or a slot of a ghost block other than block 4 (the domain's own exports).
All inputs are finite; a program needn't handle non-finite values.
Results may differ from a plain program's by a relative error of at most 0.0049.
Values may be sent and summed in bfloat16 or wider, within the bound.
A program may use at most 128 MiB of HBM per device.

v0:
```python
import functools
import math

import numpy as np
import ml_dtypes

import jax
import jax.numpy as jnp
from jax import lax
from jax.experimental import pallas as pl
from jax.experimental.pallas import tpu as pltpu
from jax.sharding import PartitionSpec as P

F32 = jnp.float32
BF = jnp.bfloat16
MESH = pl.DeviceIdType.MESH

SIDE = 16
ATOMS = 384
GHOSTS = 256
SLOTS = 32
GROUP = 16
EDGES = GROUP * SLOTS
BLOCKS = ATOMS // GROUP
EXT = ATOMS + 9 * GHOSTS
CUT = 6.25


def real_basis(count):
    n = np.arange(count)
    rows = np.zeros((count, count))
    slope = np.zeros((count, count))
    rows[0] = 1.0 / math.sqrt(count)
    rows[1] = np.where(n % 2 == 0, 1.0, -1.0) / math.sqrt(count)
    for k in range(1, count // 2):
        angle = 2.0 * math.pi * (k * n % count) / count
        rows[2 * k] = math.sqrt(2.0 / count) * np.cos(angle)
        rows[2 * k + 1] = math.sqrt(2.0 / count) * np.sin(angle)
        wave = 2.0 * math.pi * k / count
        slope[2 * k] = wave * rows[2 * k + 1]
        slope[2 * k + 1] = -wave * rows[2 * k]
    return rows, slope


def halves(table):
    high = table.astype(np.float32).astype(ml_dtypes.bfloat16)
    low = (table - high.astype(np.float64)).astype(np.float32).astype(ml_dtypes.bfloat16)
    return np.stack([high, low])


def grid_tables():
    basis, slope = real_basis(8 * SIDE)
    eye = np.eye(4)
    by = basis.reshape(SIDE, 2, 4, SIDE, 8)
    dy = slope.reshape(SIDE, 2, 4, SIDE, 8)
    y_forward = np.einsum("phkry,ab->hpkarby", by, eye).reshape(512, 512)
    y_back = np.stack(
        [
            np.einsum("phkry,ab->rayhpkb", by, eye),
            np.einsum("phkry,ab->rayhpkb", dy, eye),
        ]
    ).reshape(1024, 512)
    bx = basis.reshape(128, SIDE, 2, 4)
    dx = slope.reshape(128, SIDE, 2, 4)
    x_forward = np.einsum("sphx,ab->sapbhx", bx, eye)
    x_forward = x_forward.transpose(0, 1, 2, 4, 3, 5).reshape(512, 512)
    x_back = np.einsum("fsphx,ab->pfhbxsa", np.stack([bx, dx]), eye)
    x_back = x_back.reshape(1024, 512)
    z = np.arange(1024)
    coarse = 2.0 * math.pi * (32 * np.arange(16)[:, None] * z % 1024) / 1024
    fine = 2.0 * math.pi * (np.arange(32)[:, None] * z % 1024) / 1024
    scale = math.sqrt(2.0 / 1024)
    z_rows = np.concatenate(
        [np.cos(coarse), np.sin(coarse), scale * np.cos(fine), scale * np.sin(fine)]
    )
    return tuple(halves(t) for t in (y_forward, x_forward, x_back, y_back, z_rows))


def silu(x):
    half = 0.5 * x
    return half + half * jnp.tanh(half)


def transposed_left(a, b):
    return lax.dot_general(a, b, (((0,), (0,)), ((), ())), preferred_element_type=F32)


def transposed_right(a, b):
    return lax.dot_general(a, b, (((1,), (1,)), ((), ())), preferred_element_type=F32)


def fill_table(table, first, count, feat, pos, w_pair, shift_x, shift_y):
    flat = table.reshape(EXT * 8, 128)
    projected = jnp.dot(feat, w_pair, preferred_element_type=F32).astype(BF).astype(F32)
    lane = lax.broadcasted_iota(jnp.int32, (16, 384), 1)
    row = lax.broadcasted_iota(jnp.int32, (16, 384), 0)
    spread = (lane // 128 == row).astype(F32).astype(BF)
    xyz = transposed_left(pos, spread)
    parts = (
        projected[:, :128],
        projected[:, 128:],
        xyz[:, :128] + shift_x,
        xyz[:, 128:256] + shift_y,
        xyz[:, 256:],
    )
    for k, part in enumerate(parts):
        flat[pl.ds(first * 8 + k, count, stride=8), :] = part


def gather_edges(block, lists, table, picked, unroll):
    def one_slot(k, carry):
        for a in range(GROUP):
            j = lists[block * GROUP + a, k]
            picked[k * GROUP + a] = table[j]
        return carry

    lax.fori_loop(0, SLOTS, one_slot, 0, unroll=unroll)


def edge_block(block, table, picked, own, radial_w, expand_w, contract_w, sums):
    first = pl.multiple_of(block * GROUP, GROUP)
    picked = picked.reshape(EDGES * 8, 128)
    table = table.reshape(EXT * 8, 128)

    def far(k):
        return picked[pl.ds(k, EDGES, stride=8), :].reshape(SLOTS, GROUP, 128)

    def near(k):
        return table[pl.ds(first * 8 + k, GROUP, stride=8), :][None]

    dx, dy, dz = far(2) - near(2), far(3) - near(3), far(4) - near(4)
    d2 = dx * dx + dy * dy + dz * dz
    lane = lax.broadcasted_iota(jnp.int32, (1, 1, 128), 2)
    u = d2 * (7.0 / CUT) - (lane % 8).astype(F32)
    basis = jnp.exp(-(u * u))
    envelope = jnp.square(jnp.maximum(0.0, 1.0 - d2 * (1.0 / CUT)))
    rest = basis - basis.astype(BF).astype(F32)
    left = jnp.where((lane >= 8) & (lane < 16), rest, basis).astype(BF)
    radial = jnp.dot(
        left.reshape(EDGES, 128), radial_w[...], preferred_element_type=F32
    ).reshape(SLOTS, GROUP, 128)
    edge_in = silu(radial + own[pl.ds(first, GROUP), :][None] + far(0))
    edge_in = edge_in.astype(BF).reshape(EDGES, 128)
    half = jnp.dot(edge_in, expand_w[...], preferred_element_type=F32)
    latent = (half + half * jnp.tanh(half)).astype(BF)
    mixed = jnp.dot(latent, contract_w[...], preferred_element_type=F32)
    weight = mixed.reshape(SLOTS, GROUP, 128) * envelope * far(1)
    scale = 1.0 / math.sqrt(SLOTS)
    for i, term in enumerate((weight, dx * weight, dy * weight, dz * weight)):
        sums[i, pl.ds(first, GROUP), :] = jnp.sum(term, axis=0) * scale


def edge_forces(sums, w_final):
    scalar, vx, vy, vz = (sums[i] for i in range(4))
    invariant = (scalar + (vx * vx + vy * vy + vz * vz) / 3.0).astype(BF)
    gate = silu(jnp.dot(invariant, w_final, preferred_element_type=F32))
    ones = jnp.ones((8, 128), F32)
    rows = [
        lax.dot_general(
            ones,
            v * gate,
            (((1,), (1,)), ((), ())),
            precision=lax.Precision.HIGHEST,
            preferred_element_type=F32,
        )[0:1]
        for v in (vx, vy, vz)
    ]
    return [row * (1.0 / math.sqrt(128.0)) for row in rows]


def two_halves(table, right):
    return jnp.dot(table[0], right, preferred_element_type=F32) + jnp.dot(
        table[1], right, preferred_element_type=F32
    )


def swap_halves(low, high):
    lane = lax.broadcasted_iota(jnp.int32, low.shape, low.ndim - 1)
    first = lane < 64
    turned_high = pltpu.roll(high, 64, high.ndim - 1)
    turned_low = pltpu.roll(low, 64, low.ndim - 1)
    return jnp.where(first, low, turned_high), jnp.where(first, turned_low, high)


def green_block(px, ry):
    row = lax.broadcasted_iota(jnp.int32, (512, 128), 0)
    lane = lax.broadcasted_iota(jnp.int32, (512, 128), 1)
    x_slot = row // 4
    y_slot = px * 8 + (lane // 64) * 4 + row % 4
    c = lane % 64
    x_mode = jnp.where(x_slot == 1, 64, x_slot // 2)
    y_mode = jnp.where(y_slot == 1, 64, y_slot // 2)
    z_mode = jnp.where((c == 32) & (ry == 0), 512, ry * 32 + c % 32)
    kx = x_mode.astype(F32) * (2.0 * math.pi / 128)
    ky = y_mode.astype(F32) * (2.0 * math.pi / 128)
    kz = z_mode.astype(F32) * (2.0 * math.pi / 1024)
    kk = kx * kx + ky * ky + kz * kz
    zero = (x_mode == 0) & (y_mode == 0) & (z_mode == 0)
    safe = jnp.where(zero, 1.0, kk)
    return jnp.where(zero, 0.0, 4.0 * math.pi * jnp.exp(-0.5 * kk) / safe)


class Exchange:
    def __init__(self, axis, outgoing, landing, send_sems, recv_sems):
        self.axis = axis
        self.outgoing, self.landing = outgoing, landing
        self.send_sems, self.recv_sems = send_sems, recv_sems
        self.me = lax.axis_index(axis)

    def copy(self, step, target, slot):
        return pltpu.make_async_remote_copy(
            src_ref=self.outgoing.at[target],
            dst_ref=self.landing.at[slot],
            send_sem=self.send_sems.at[step],
            recv_sem=self.recv_sems.at[step],
            device_id={self.axis: target},
            device_id_type=MESH,
        )

    def start(self):
        def one(step, carry):
            target = lax.rem(self.me + step, SIDE)
            self.copy(step, target, self.me).start()
            return carry

        lax.fori_loop(1, SIDE, one, 0)
        self.landing[pl.ds(self.me, 1)] = self.outgoing[pl.ds(self.me, 1)]

    def wait_recv(self):
        def one(step, carry):
            target = lax.rem(self.me + step, SIDE)
            source = lax.rem(self.me - step + SIDE, SIDE)
            self.copy(step, target, source).wait_recv()
            return carry

        lax.fori_loop(1, SIDE, one, 0)

    def wait_send(self):
        def one(step, carry):
            target = lax.rem(self.me + step, SIDE)
            self.copy(step, target, self.me).wait_send()
            return carry

        lax.fori_loop(1, SIDE, one, 0)


GHOST_BLOCKS = tuple(b for b in range(9) if b != 4)


def device_kernel(
    lists,
    count,
    feat,
    positions,
    exports,
    cells,
    w_self,
    w_pair,
    w_radial,
    w_expand,
    w_contract,
    w_final,
    w_charge,
    y_forward,
    x_forward,
    x_back,
    y_back,
    z_rows,
    out,
    table,
    picked_even,
    picked_odd,
    own,
    radial_w,
    expand_w,
    sums,
    pos16,
    out_feat,
    out_pos,
    ghost_feat,
    ghost_pos,
    z_basis,
    send1,
    land1,
    send2,
    land2,
    send3,
    land3,
    send4,
    land4,
    sems,
    halo_sems,
):
    px = lax.axis_index("dx")
    ry = lax.axis_index("dy")
    barrier = pltpu.get_barrier_semaphore()

    def greet(step, carry):
        pl.semaphore_signal(
            barrier,
            inc=1,
            device_id={"dx": lax.rem(px + step, SIDE), "dy": ry},
            device_id_type=MESH,
        )
        pl.semaphore_signal(
            barrier,
            inc=1,
            device_id={"dx": px, "dy": lax.rem(ry + step, SIDE)},
            device_id_type=MESH,
        )
        return carry

    lax.fori_loop(1, SIDE, greet, 0)
    for a in (1, SIDE - 1):
        for b in (1, SIDE - 1):
            pl.semaphore_signal(
                barrier,
                inc=1,
                device_id={"dx": lax.rem(px + a, SIDE), "dy": lax.rem(ry + b, SIDE)},
                device_id_type=MESH,
            )

    pos16[...] = jnp.zeros_like(pos16)
    pos16[0:3, :] = positions[...].astype(F32)
    pos = pos16[...].astype(BF)
    slot = lax.broadcasted_iota(jnp.int32, (ATOMS, GHOSTS), 0)
    chosen = (slot == exports[...]).astype(F32).astype(BF)
    out_feat[...] = transposed_left(chosen, feat[...]).astype(BF)
    out_pos[...] = jnp.dot(pos, chosen, preferred_element_type=F32).astype(BF)

    cell = cells[...]
    height = cell % 1024
    column = cell // 1024
    level = lax.broadcasted_iota(jnp.int32, (1024, ATOMS), 0)
    at_height = (level == height).astype(F32).astype(BF)
    angles = two_halves(z_rows, at_height)
    fine_cos, fine_sin = angles[32:64], angles[64:96]
    root = math.sqrt(0.5)
    fine_row = lax.broadcasted_iota(jnp.int32, (32, ATOMS), 0)
    alternate = jnp.where(height % 2 == 0, 1.0, -1.0) * math.sqrt(1.0 / 1024)
    for r in range(SIDE):
        big_cos, big_sin = angles[r : r + 1], angles[16 + r : 17 + r]
        cosine = big_cos * fine_cos - big_sin * fine_sin
        sine = big_sin * fine_cos + big_cos * fine_sin
        if r == 0:
            cosine = jnp.where(fine_row == 0, cosine * root, cosine)
            sine = jnp.where(fine_row == 0, alternate, sine)
        z_basis[64 * r : 64 * r + 32, :] = cosine
        z_basis[64 * r + 32 : 64 * r + 64, :] = sine

    charge_w = jnp.broadcast_to(w_charge[...], (8, 128))
    atom = lax.broadcasted_iota(jnp.int32, (1, ATOMS), 1)
    live = atom < count[0, 0]
    charge = jnp.where(live, transposed_right(charge_w, feat[...])[0:1], 0.0)
    place = lax.broadcasted_iota(jnp.int32, (64, ATOMS), 0)
    at_column = (place == column).astype(F32).astype(BF)
    loaded = z_basis[...] * charge
    loaded_high = loaded.astype(BF)
    loaded_low = (loaded - loaded_high.astype(F32)).astype(BF)
    density = transposed_right(at_column, loaded_high) + transposed_right(at_column, loaded_low)
    for q in range(8):
        part = density[:, 128 * q : 128 * q + 128]
        even, odd = swap_halves(part[:32], part[32:])
        send1[2 * q] = even.astype(BF)
        send1[2 * q + 1] = odd.astype(BF)

    pl.semaphore_wait(barrier, 34)
    over_y = Exchange("dy", send1, land1, sems.at[0], sems.at[1])
    over_x = Exchange("dx", send2, land2, sems.at[2], sems.at[3])
    back_x = Exchange("dx", send3, land3, sems.at[4], sems.at[5])
    back_y = Exchange("dy", send4, land4, sems.at[6], sems.at[7])
    over_y.start()
    halo = []
    for i, b in enumerate(GHOST_BLOCKS):
        target = {
            "dx": lax.rem(px + SIDE + 1 - b // 3, SIDE),
            "dy": lax.rem(ry + SIDE + 1 - b % 3, SIDE),
        }
        for j, (source, landing) in enumerate(((out_feat, ghost_feat), (out_pos, ghost_pos))):
            copy = pltpu.make_async_remote_copy(
                src_ref=source,
                dst_ref=landing.at[b],
                send_sem=halo_sems.at[j, i],
                recv_sem=halo_sems.at[2 + j, i],
                device_id=target,
                device_id_type=MESH,
            )
            copy.start()
            halo.append(copy)

    w_rad = w_radial[...]
    rad_high = w_rad.astype(BF).astype(F32)
    stacked = jnp.concatenate(
        [rad_high, rad_high, w_rad - rad_high, jnp.zeros((104, 128), F32)], axis=0
    )
    radial_w[...] = stacked.astype(BF)
    expand_w[...] = (w_expand[...].astype(F32) * 0.5).astype(BF)
    own[...] = jnp.dot(feat[...], w_self[...], preferred_element_type=F32)
    fill_table(table, 0, ATOMS, feat[...], pos, w_pair[...], 0.0, 0.0)
    green = green_block(px, ry)

    over_y.wait_recv()
    along_y = two_halves(y_forward, land1[...].reshape(512, 128))
    low, high = swap_halves(along_y[:256], along_y[256:])
    send2[:, 0:16, :] = low.astype(BF).reshape(SIDE, 16, 128)
    send2[:, 16:32, :] = high.astype(BF).reshape(SIDE, 16, 128)
    over_x.start()

    for copy in halo:
        copy.wait_recv()
    for b in GHOST_BLOCKS:
        fill_table(
            table,
            ATOMS + GHOSTS * b,
            GHOSTS,
            ghost_feat[b],
            ghost_pos[b],
            w_pair[...],
            b // 3 - 1.0,
            b % 3 - 1.0,
        )

    def edges(start, stop):
        fixed = (own, radial_w, expand_w, w_contract, sums)

        def pair(h, carry):
            block = 2 * h
            gather_edges(block + 1, lists, table, picked_odd, SLOTS)
            edge_block(block, table, picked_even, *fixed)
            following = jnp.minimum(block + 2, BLOCKS - 1)
            gather_edges(following, lists, table, picked_even, SLOTS)
            edge_block(block + 1, table, picked_odd, *fixed)
            return carry

        lax.fori_loop(start // 2, stop // 2, pair, 0)

    over_x.wait_recv()
    spectrum = two_halves(x_forward, land2[...].reshape(512, 128)) * green
    top = spectrum.astype(BF)
    rest = (spectrum - top.astype(F32)).astype(BF)
    along_x = two_halves(x_back, top) + jnp.dot(x_back[0], rest, preferred_element_type=F32)
    send3[...] = along_x.astype(BF).reshape(SIDE, 64, 128)
    back_x.start()
    gather_edges(0, lists, table, picked_even, 1)
    edges(0, BLOCKS // 3)

    back_x.wait_recv()
    arrived = []
    for f in range(2):
        low = land3[:, 32 * f : 32 * f + 16, :].astype(F32).reshape(256, 128)
        high = land3[:, 32 * f + 16 : 32 * f + 32, :].astype(F32).reshape(256, 128)
        low, high = swap_halves(low, high)
        arrived.append(jnp.concatenate([low, high], axis=0).astype(BF))
    from_potential = two_halves(y_back, arrived[0]).astype(BF).reshape(2, SIDE, 32, 128)
    from_slope = (
        jnp.dot(y_back[0, 0:512], arrived[1], preferred_element_type=F32)
        + jnp.dot(y_back[1, 0:512], arrived[1], preferred_element_type=F32)
    )
    send4[:, 0:32, :] = from_potential[0]
    send4[:, 32:64, :] = from_slope.astype(BF).reshape(SIDE, 32, 128)
    send4[:, 64:96, :] = from_potential[1]
    back_y.start()
    edges(BLOCKS // 3, BLOCKS)
    short = edge_forces(sums, w_final[...])

    back_y.wait_recv()
    fields = []
    for f in range(3):
        lows, highs = [], []
        for q in range(8):
            low, high = swap_halves(
                land4[2 * q, 32 * f : 32 * f + 32, :].astype(F32),
                land4[2 * q + 1, 32 * f : 32 * f + 32, :].astype(F32),
            )
            lows.append(low)
            highs.append(high)
        coefficients = jnp.concatenate(
            [jnp.concatenate(lows, axis=1), jnp.concatenate(highs, axis=1)], axis=0
        ).astype(BF)
        fields.append(transposed_left(coefficients, at_column))
    potential, slope_x, slope_y = fields
    values = z_basis[...]
    field_x = jnp.sum(slope_x * values, axis=0, keepdims=True)
    field_y = jnp.sum(slope_y * values, axis=0, keepdims=True)
    pairs = potential.reshape(SIDE, 64, ATOMS)
    basis = values.reshape(SIDE, 64, ATOMS)
    wave = (
        lax.broadcasted_iota(jnp.int32, (SIDE, 32, ATOMS), 0) * 32
        + lax.broadcasted_iota(jnp.int32, (SIDE, 32, ATOMS), 1)
    ).astype(F32) * (2.0 * math.pi / 1024)
    turned = wave * (pairs[:, :32] * basis[:, 32:] - pairs[:, 32:] * basis[:, :32])
    field_z = jnp.sum(turned.reshape(512, ATOMS), axis=0, keepdims=True)
    for a, field in enumerate((field_x, field_y, field_z)):
        out[a : a + 1, :] = jnp.where(live, short[a] + charge * field, 0.0)

    for copy in halo:
        copy.wait_send()
    for exchange in (over_y, over_x, back_x, back_y):
        exchange.wait_send()


def shards(
    features,
    positions,
    atom_count,
    ghost_index,
    neighbour_list,
    cell_index,
    w_self,
    w_pair,
    w_radial,
    w_expand,
    w_contract,
    w_final,
    w_charge,
):
    tables = [jnp.asarray(t) for t in grid_tables()]
    vmem = pl.BlockSpec(memory_space=pltpu.VMEM)
    smem = pl.BlockSpec(memory_space=pltpu.SMEM)
    forces = pl.pallas_call(
        device_kernel,
        out_shape=jax.ShapeDtypeStruct((3, ATOMS), F32),
        in_specs=[smem, smem] + [vmem] * 16,
        out_specs=vmem,
        scratch_shapes=[
            pltpu.VMEM((EXT, 8, 128), F32),
            pltpu.VMEM((EDGES, 8, 128), F32),
            pltpu.VMEM((EDGES, 8, 128), F32),
            pltpu.VMEM((ATOMS, 128), F32),
            pltpu.VMEM((128, 128), BF),
            pltpu.VMEM((128, 1024), BF),
            pltpu.VMEM((4, ATOMS, 128), F32),
            pltpu.VMEM((16, ATOMS), F32),
            pltpu.VMEM((GHOSTS, 128), BF),
            pltpu.VMEM((16, GHOSTS), BF),
            pltpu.VMEM((9, GHOSTS, 128), BF),
            pltpu.VMEM((9, 16, GHOSTS), BF),
            pltpu.VMEM((1024, ATOMS), F32),
            pltpu.VMEM((SIDE, 32, 128), BF),
            pltpu.VMEM((SIDE, 32, 128), BF),
            pltpu.VMEM((SIDE, 32, 128), BF),
            pltpu.VMEM((SIDE, 32, 128), BF),
            pltpu.VMEM((SIDE, 64, 128), BF),
            pltpu.VMEM((SIDE, 64, 128), BF),
            pltpu.VMEM((SIDE, 96, 128), BF),
            pltpu.VMEM((SIDE, 96, 128), BF),
            pltpu.SemaphoreType.DMA((8, SIDE)),
            pltpu.SemaphoreType.DMA((4, 8)),
        ],
        compiler_params=pltpu.CompilerParams(
            collective_id=0, has_side_effects=True, vmem_limit_bytes=58 * 2**20
        ),
        name="forces",
    )(
        neighbour_list[0, 0],
        atom_count,
        features[0, 0],
        positions[0, 0],
        ghost_index[0],
        cell_index[0],
        w_self,
        w_pair,
        w_radial,
        w_expand,
        w_contract,
        w_final,
        w_charge[None],
        *tables,
    )
    return forces[None, None]


def solution(mesh):
    whole = P()
    placed = (
        P("dx", "dy", None, None),
        P("dx", "dy", None, None),
        P("dx", "dy"),
        P("dx", "dy", None),
        P("dx", "dy", None, None),
        P("dx", "dy", None),
    ) + (whole,) * 7
    return jax.shard_map(
        shards, mesh=mesh, in_specs=placed, out_specs=P("dx", "dy", None, None), check_vma=False
    )
```

profile of v0, /device:TPU:1, one launch (start us, length us, event | category | flops | bytes accessed | tf_op | source)
XLA Modules:
  0.0 74.7 jit_solution(331242767057625044)
XLA Ops:
  0.7 1.6 %copy.19 = s32[1,1,384,32]{3,2,1,0:T(8,128)} copy(s32[1,1,384,32]{2,3,1,0:T(8,128)} %param.22) | data formatting | bytes 98304 | tf_op args[4]
  2.3 71.2 %forces.1 = f32[3,384]{1,0:T(4,128)} custom-call(s32[384,32]{1,0:T(8,128)} %bitcast.7, s32[1,1]{1,0:T(1,128)S(6)} %copy.21.count, bf16[384,128]{1,0:T(8,128)(2,1)} %bitcast.8, bf16[3,384]{1,0:T(4,128)(2,1)} %bitcast.10, s32[1,256]{1,0:T(1,128)} %bitcast.12, s32[1,384]{1,0:T(1,128)} %bitcast.11, bf16[128,128]{1,0:T(8,128)(2,1)} %w_self.1, ...), custom_call_target="tpu_custom_call" | custom-call | tf_op jit(solution)/shard_map/forces/pallas_call | solution.py:520
  73.4 1.3 %copy.20 = f32[1,1,3,384]{3,1,2,0:T(1,128)} copy(f32[1,1,3,384]{3,2,1,0:T(4,128)} %bitcast.9) | data formatting | bytes 9216 | tf_op jit(solution)/shard_map/broadcast_in_dim | solution.py:570
where the time goes:
time: 75.1 us; the launch traced here: 74.7 us
  Pallas kernels  71.2 us (95%)
  local copies, waits for them, and re-layouts  2.89 us (4%)
    pallas_call x1, Pallas kernels, shards(): pl.pallas_call(device_kernel, out_shape=jax.ShapeDtypeStruct((3, ATOMS),...  71.2 us
    unnamed x1, local copies, waits for them, and re-layouts  1.6 us

commit v1 on v0

--- a/solution.py
+++ b/solution.py
@@ -22,6 +22,7 @@
 GROUP = 16
 EDGES = GROUP * SLOTS
 BLOCKS = ATOMS // GROUP
+SHARES = ((0, 4), (4, 12), (12, 24))
 EXT = ATOMS + 9 * GHOSTS
 CUT = 6.25
 
@@ -108,9 +109,11 @@
 
 
 def gather_edges(block, lists, table, picked, unroll):
+    start = block * GROUP
+
     def one_slot(k, carry):
         for a in range(GROUP):
-            j = lists[block * GROUP + a, k]
+            j = lists[start + k * ATOMS + a]
             picked[k * GROUP + a] = table[j]
         return carry
 
@@ -201,18 +204,18 @@
 
 
 class Exchange:
-    def __init__(self, axis, outgoing, landing, send_sems, recv_sems):
+    def __init__(self, axis, outgoing, landing, sems):
         self.axis = axis
         self.outgoing, self.landing = outgoing, landing
-        self.send_sems, self.recv_sems = send_sems, recv_sems
+        self.send_sem, self.recv_sem = sems.at[0], sems.at[1]
         self.me = lax.axis_index(axis)
 
-    def copy(self, step, target, slot):
+    def copy(self, source, landing, target):
         return pltpu.make_async_remote_copy(
-            src_ref=self.outgoing.at[target],
-            dst_ref=self.landing.at[slot],
-            send_sem=self.send_sems.at[step],
-            recv_sem=self.recv_sems.at[step],
+            src_ref=source,
+            dst_ref=landing,
+            send_sem=self.send_sem,
+            recv_sem=self.recv_sem,
             device_id={self.axis: target},
             device_id_type=MESH,
         )
@@ -220,35 +223,28 @@
     def start(self):
         def one(step, carry):
             target = lax.rem(self.me + step, SIDE)
-            self.copy(step, target, self.me).start()
+            self.copy(self.outgoing.at[target], self.landing.at[self.me], target).start()
             return carry
 
-        lax.fori_loop(1, SIDE, one, 0)
-        self.landing[pl.ds(self.me, 1)] = self.outgoing[pl.ds(self.me, 1)]
+        lax.fori_loop(1, SIDE, one, 0, unroll=SIDE - 1)
+        self.landing[self.me] = self.outgoing[self.me]
+
+    def all_others(self):
+        others = pl.ds(0, SIDE - 1)
+        target = lax.rem(self.me + 1, SIDE)
+        return self.copy(self.outgoing.at[others], self.landing.at[others], target)
 
     def wait_recv(self):
-        def one(step, carry):
-            target = lax.rem(self.me + step, SIDE)
-            source = lax.rem(self.me - step + SIDE, SIDE)
-            self.copy(step, target, source).wait_recv()
-            return carry
-
-        lax.fori_loop(1, SIDE, one, 0)
+        self.all_others().wait_recv()
 
     def wait_send(self):
-        def one(step, carry):
-            target = lax.rem(self.me + step, SIDE)
-            self.copy(step, target, self.me).wait_send()
-            return carry
-
-        lax.fori_loop(1, SIDE, one, 0)
-
-
-GHOST_BLOCKS = tuple(b for b in range(9) if b != 4)
+        self.all_others().wait_send()
+
+
+GHOST_BLOCKS = (3, 5, 1, 7, 0, 2, 6, 8)
 
 
 def device_kernel(
-    lists,
     count,
     feat,
     positions,
@@ -257,16 +253,25 @@
     w_self,
     w_pair,
     w_radial,
-    w_expand,
-    w_contract,
     w_final,
     w_charge,
+    z_rows_far,
+    w_expand_far,
+    lists_far,
+    y_forward_far,
+    w_contract_far,
+    x_forward_far,
+    x_back_far,
+    y_back_far,
+    out,
+    z_rows,
+    w_expand,
+    lists,
     y_forward,
+    w_contract,
     x_forward,
     x_back,
     y_back,
-    z_rows,
-    out,
     table,
     picked_even,
     picked_odd,
@@ -288,8 +293,10 @@
     land3,
     send4,
     land4,
+    green,
     sems,
     halo_sems,
+    load_sems,
 ):
     px = lax.axis_index("dx")
     ry = lax.axis_index("dy")
@@ -320,6 +327,24 @@
                 device_id_type=MESH,
             )
 
+    loads = [
+        pltpu.make_async_copy(far, near, load_sems.at[i])
+        for i, (far, near) in enumerate(
+            (
+                (z_rows_far, z_rows),
+                (w_expand_far, w_expand),
+                (y_forward_far, y_forward),
+                (w_contract_far, w_contract),
+                (x_forward_far, x_forward),
+                (x_back_far, x_back),
+                (y_back_far, y_back),
+            )
+            + ((lists_far, lists),)
+        )
+    ]
+    for load in loads:
+        load.start()
+
     pos16[...] = jnp.zeros_like(pos16)
     pos16[0:3, :] = positions[...].astype(F32)
     pos = pos16[...].astype(BF)
@@ -333,6 +358,7 @@
     column = cell // 1024
     level = lax.broadcasted_iota(jnp.int32, (1024, ATOMS), 0)
     at_height = (level == height).astype(F32).astype(BF)
+    loads[0].wait()
     angles = two_halves(z_rows, at_height)
     fine_cos, fine_sin = angles[32:64], angles[64:96]
     root = math.sqrt(0.5)
@@ -364,13 +390,26 @@
         send1[2 * q] = even.astype(BF)
         send1[2 * q + 1] = odd.astype(BF)
 
+
+    w_rad = w_radial[...]
+    rad_high = w_rad.astype(BF).astype(F32)
+    stacked = jnp.concatenate(
+        [rad_high, rad_high, w_rad - rad_high, jnp.zeros((104, 128), F32)], axis=0
+    )
+    radial_w[...] = stacked.astype(BF)
+    loads[1].wait()
+    expand_w[...] = (w_expand[...].astype(F32) * 0.5).astype(BF)
+    own[...] = jnp.dot(feat[...], w_self[...], preferred_element_type=F32)
+    fill_table(table, 0, ATOMS, feat[...], pos, w_pair[...], 0.0, 0.0)
+    green[...] = green_block(px, ry)
+
     pl.semaphore_wait(barrier, 34)
-    over_y = Exchange("dy", send1, land1, sems.at[0], sems.at[1])
-    over_x = Exchange("dx", send2, land2, sems.at[2], sems.at[3])
-    back_x = Exchange("dx", send3, land3, sems.at[4], sems.at[5])
-    back_y = Exchange("dy", send4, land4, sems.at[6], sems.at[7])
+    over_y = Exchange("dy", send1, land1, sems.at[0])
+    over_x = Exchange("dx", send2, land2, sems.at[1])
+    back_x = Exchange("dx", send3, land3, sems.at[2])
+    back_y = Exchange("dy", send4, land4, sems.at[3])
     over_y.start()
-    halo = []
+    halo = {}
     for i, b in enumerate(GHOST_BLOCKS):
         target = {
             "dx": lax.rem(px + SIDE + 1 - b // 3, SIDE),
@@ -386,29 +425,19 @@
                 device_id_type=MESH,
             )
             copy.start()
-            halo.append(copy)
-
-    w_rad = w_radial[...]
-    rad_high = w_rad.astype(BF).astype(F32)
-    stacked = jnp.concatenate(
-        [rad_high, rad_high, w_rad - rad_high, jnp.zeros((104, 128), F32)], axis=0
-    )
-    radial_w[...] = stacked.astype(BF)
-    expand_w[...] = (w_expand[...].astype(F32) * 0.5).astype(BF)
-    own[...] = jnp.dot(feat[...], w_self[...], preferred_element_type=F32)
-    fill_table(table, 0, ATOMS, feat[...], pos, w_pair[...], 0.0, 0.0)
-    green = green_block(px, ry)
+            halo[b, j] = copy
 
     over_y.wait_recv()
+    loads[2].wait()
     along_y = two_halves(y_forward, land1[...].reshape(512, 128))
     low, high = swap_halves(along_y[:256], along_y[256:])
     send2[:, 0:16, :] = low.astype(BF).reshape(SIDE, 16, 128)
     send2[:, 16:32, :] = high.astype(BF).reshape(SIDE, 16, 128)
     over_x.start()
 
-    for copy in halo:
-        copy.wait_recv()
     for b in GHOST_BLOCKS:
+        halo[b, 0].wait_recv()
+        halo[b, 1].wait_recv()
         fill_table(
             table,
             ATOMS + GHOSTS * b,
@@ -434,17 +463,24 @@
 
         lax.fori_loop(start // 2, stop // 2, pair, 0)
 
+    for i in (3, 7):
+        loads[i].wait()
+    gather_edges(0, lists, table, picked_even, 1)
+    edges(*SHARES[0])
+
     over_x.wait_recv()
-    spectrum = two_halves(x_forward, land2[...].reshape(512, 128)) * green
+    loads[4].wait()
+    loads[5].wait()
+    spectrum = two_halves(x_forward, land2[...].reshape(512, 128)) * green[...]
     top = spectrum.astype(BF)
     rest = (spectrum - top.astype(F32)).astype(BF)
     along_x = two_halves(x_back, top) + jnp.dot(x_back[0], rest, preferred_element_type=F32)
     send3[...] = along_x.astype(BF).reshape(SIDE, 64, 128)
     back_x.start()
-    gather_edges(0, lists, table, picked_even, 1)
-    edges(0, BLOCKS // 3)
+    edges(*SHARES[1])
 
     back_x.wait_recv()
+    loads[6].wait()
     arrived = []
     for f in range(2):
         low = land3[:, 32 * f : 32 * f + 16, :].astype(F32).reshape(256, 128)
@@ -460,7 +496,7 @@
     send4[:, 32:64, :] = from_slope.astype(BF).reshape(SIDE, 32, 128)
     send4[:, 64:96, :] = from_potential[1]
     back_y.start()
-    edges(BLOCKS // 3, BLOCKS)
+    edges(*SHARES[2])
     short = edge_forces(sums, w_final[...])
 
     back_y.wait_recv()
@@ -493,7 +529,7 @@
     for a, field in enumerate((field_x, field_y, field_z)):
         out[a : a + 1, :] = jnp.where(live, short[a] + charge * field, 0.0)
 
-    for copy in halo:
+    for copy in halo.values():
         copy.wait_send()
     for exchange in (over_y, over_x, back_x, back_y):
         exchange.wait_send()
@@ -514,15 +550,24 @@
     w_final,
     w_charge,
 ):
-    tables = [jnp.asarray(t) for t in grid_tables()]
+    y_forward, x_forward, x_back, y_back, z_rows = (jnp.asarray(t) for t in grid_tables())
     vmem = pl.BlockSpec(memory_space=pltpu.VMEM)
     smem = pl.BlockSpec(memory_space=pltpu.SMEM)
+    far = pl.BlockSpec(memory_space=pl.ANY)
     forces = pl.pallas_call(
         device_kernel,
         out_shape=jax.ShapeDtypeStruct((3, ATOMS), F32),
-        in_specs=[smem, smem] + [vmem] * 16,
+        in_specs=[smem] + [vmem] * 9 + [far] * 8,
         out_specs=vmem,
         scratch_shapes=[
+            pltpu.VMEM((2, 96, 1024), BF),
+            pltpu.VMEM((128, 1024), BF),
+            pltpu.SMEM((SLOTS * ATOMS,), jnp.int32),
+            pltpu.VMEM((2, 512, 512), BF),
+            pltpu.VMEM((1024, 128), BF),
+            pltpu.VMEM((2, 512, 512), BF),
+            pltpu.VMEM((2, 1024, 512), BF),
+            pltpu.VMEM((2, 1024, 512), BF),
             pltpu.VMEM((EXT, 8, 128), F32),
             pltpu.VMEM((EDGES, 8, 128), F32),
             pltpu.VMEM((EDGES, 8, 128), F32),
@@ -544,15 +589,16 @@
             pltpu.VMEM((SIDE, 64, 128), BF),
             pltpu.VMEM((SIDE, 96, 128), BF),
             pltpu.VMEM((SIDE, 96, 128), BF),
-            pltpu.SemaphoreType.DMA((8, SIDE)),
+            pltpu.VMEM((512, 128), F32),
+            pltpu.SemaphoreType.DMA((4, 2)),
             pltpu.SemaphoreType.DMA((4, 8)),
+            pltpu.SemaphoreType.DMA((8,)),
         ],
         compiler_params=pltpu.CompilerParams(
             collective_id=0, has_side_effects=True, vmem_limit_bytes=58 * 2**20
         ),
         name="forces",
     )(
-        neighbour_list[0, 0],
         atom_count,
         features[0, 0],
         positions[0, 0],
@@ -561,11 +607,16 @@
         w_self,
         w_pair,
         w_radial,
-        w_expand,
-        w_contract,
         w_final,
         w_charge[None],
-        *tables,
+        z_rows,
+        w_expand,
+        neighbour_list[0, 0].T.reshape(-1),
+        y_forward,
+        w_contract,
+        x_forward,
+        x_back,
+        y_back,
     )
     return forces[None, None]
 

time: 75.1 us -> 69.7 us (0.928)
  Pallas kernels: 71.2 us -> 66.2 us
    pallas_call x1, Pallas kernels: 71.2 us -> 66.2 us  [shards(): pl.pallas_call(device_kernel, out_shape=jax.ShapeDtypeStruct((3, ATOMS),...]
    unnamed x1 -> x0, local copies, waits for them, and re-layouts: 1.6 us -> none
    reshape x0 -> x1, local copies, waits for them, and re-layouts: none -> 1.42 us  [shards(): neighbour_list[0, 0].T.reshape(-1)]
where the time goes in v1:
time: 69.7 us; the launch traced here: 69.5 us
  Pallas kernels  66.2 us (95%)
  local copies, waits for them, and re-layouts  2.71 us (4%)
    pallas_call x1, Pallas kernels, shards(): pl.pallas_call(device_kernel, out_shape=jax.ShapeDtypeStruct((3, ATOMS),...  66.2 us
    reshape x1, local copies, waits for them, and re-layouts, shards(): neighbour_list[0, 0].T.reshape(-1)  1.42 us

profile of v1, /device:TPU:1, one launch (start us, length us, event | category | flops | bytes accessed | tf_op | source)
XLA Modules:
  0.0 69.5 jit_solution(10647299279215058478)
XLA Ops:
  0.7 1.4 %reshape.3.lists_far = s32[12288]{0:T(1024)} reshape(s32[32,384]{1,0:T(8,128)} %bitcast.10) | data formatting | bytes 98304 | tf_op jit(solution)/shard_map/reshape | solution.py:614
  2.1 66.2 %forces.1 = f32[3,384]{1,0:T(4,128)} custom-call(s32[1,1]{1,0:T(1,128)S(6)} %copy.20.count, bf16[384,128]{1,0:T(8,128)(2,1)} %bitcast.9, bf16[3,384]{1,0:T(4,128)(2,1)} %bitcast.12, s32[1,256]{1,0:T(1,128)} %bitcast.14, s32[1,384]{1,0:T(1,128)} %bitcast.13, bf16[128,128]{1,0:T(8,128)(2,1)} %w_self.1, bf16[128,256]{1,0:T(8,128)(2,1)} %w_pair.1, ...), custom_call_target="tpu_custom_call" | custom-call | tf_op jit(solution)/shard_map/forces/pallas_call | solution.py:557
  68.2 1.3 %copy.19 = f32[1,1,3,384]{3,1,2,0:T(1,128)} copy(f32[1,1,3,384]{3,2,1,0:T(4,128)} %bitcast.11) | data formatting | bytes 9216 | tf_op jit(solution)/shard_map/broadcast_in_dim | solution.py:621

commit v2 on v1

--- a/solution.py
+++ b/solution.py
@@ -22,7 +22,8 @@
 GROUP = 16
 EDGES = GROUP * SLOTS
 BLOCKS = ATOMS // GROUP
-SHARES = ((0, 4), (4, 12), (12, 24))
+PIECE = 256
+SHARES = ((0, 6), (6, 14), (14, 24))
 EXT = ATOMS + 9 * GHOSTS
 CUT = 6.25
 
@@ -108,25 +109,28 @@
         flat[pl.ds(first * 8 + k, count, stride=8), :] = part
 
 
-def gather_edges(block, lists, table, picked, unroll):
+def gather_edges(block, first, count, lists, table, picked, unroll):
     start = block * GROUP
 
-    def one_slot(k, carry):
+    def one_slot(i, carry):
+        k = first + i
         for a in range(GROUP):
             j = lists[start + k * ATOMS + a]
             picked[k * GROUP + a] = table[j]
         return carry
 
-    lax.fori_loop(0, SLOTS, one_slot, 0, unroll=unroll)
-
-
-def edge_block(block, table, picked, own, radial_w, expand_w, contract_w, sums):
+    lax.fori_loop(0, count, one_slot, 0, unroll=unroll)
+
+
+def edge_inputs(block, slot, count, table, picked, own, radial_w, hidden, gains):
     first = pl.multiple_of(block * GROUP, GROUP)
+    rows = count * GROUP
     picked = picked.reshape(EDGES * 8, 128)
     table = table.reshape(EXT * 8, 128)
 
     def far(k):
-        return picked[pl.ds(k, EDGES, stride=8), :].reshape(SLOTS, GROUP, 128)
+        start = slot * GROUP * 8 + k
+        return picked[pl.ds(start, rows, stride=8), :].reshape(count, GROUP, 128)
 
     def near(k):
         return table[pl.ds(first * 8 + k, GROUP, stride=8), :][None]
@@ -140,17 +144,34 @@
     rest = basis - basis.astype(BF).astype(F32)
     left = jnp.where((lane >= 8) & (lane < 16), rest, basis).astype(BF)
     radial = jnp.dot(
-        left.reshape(EDGES, 128), radial_w[...], preferred_element_type=F32
-    ).reshape(SLOTS, GROUP, 128)
+        left.reshape(rows, 128), radial_w[...], preferred_element_type=F32
+    ).reshape(count, GROUP, 128)
     edge_in = silu(radial + own[pl.ds(first, GROUP), :][None] + far(0))
-    edge_in = edge_in.astype(BF).reshape(EDGES, 128)
-    half = jnp.dot(edge_in, expand_w[...], preferred_element_type=F32)
-    latent = (half + half * jnp.tanh(half)).astype(BF)
-    mixed = jnp.dot(latent, contract_w[...], preferred_element_type=F32)
-    weight = mixed.reshape(SLOTS, GROUP, 128) * envelope * far(1)
-    scale = 1.0 / math.sqrt(SLOTS)
-    for i, term in enumerate((weight, dx * weight, dy * weight, dz * weight)):
-        sums[i, pl.ds(first, GROUP), :] = jnp.sum(term, axis=0) * scale
+    hidden[slot * GROUP : slot * GROUP + rows] = edge_in.astype(BF).reshape(rows, 128)
+    gain = envelope * far(1)
+    for i, term in enumerate((gain, dx * gain, dy * gain, dz * gain)):
+        gains[i, slot : slot + count] = term
+
+
+def edge_step(block, lists, table, picked, hidden, gains, own, radial_w, expand_w, contract_w, sums):
+    last = BLOCKS - 1
+    totals = None
+    for m in range(0, EDGES, PIECE):
+        slot, count = m // GROUP, PIECE // GROUP
+        gather_edges(jnp.minimum(block + 2, last), slot, count, lists, table, picked[0], count)
+        following = jnp.minimum(block + 1, last)
+        edge_inputs(
+            following, slot, count, table, picked[1], own, radial_w, hidden[1], gains[1]
+        )
+        half = jnp.dot(hidden[0][m : m + PIECE], expand_w[...], preferred_element_type=F32)
+        latent = (half + half * jnp.tanh(half)).astype(BF)
+        mixed = jnp.dot(latent, contract_w[...], preferred_element_type=F32)
+        mixed = mixed.reshape(count, GROUP, 128)
+        part = [jnp.sum(mixed * gains[0][i, slot : slot + count], axis=0) for i in range(4)]
+        totals = part if totals is None else [x + y for x, y in zip(totals, part)]
+    first = pl.multiple_of(block * GROUP, GROUP)
+    for i in range(4):
+        sums[i, pl.ds(first, GROUP), :] = totals[i] * (1.0 / math.sqrt(SLOTS))
 
 
 def edge_forces(sums, w_final):
@@ -275,6 +296,10 @@
     table,
     picked_even,
     picked_odd,
+    hidden_even,
+    hidden_odd,
+    gains_even,
+    gains_odd,
     own,
     radial_w,
     expand_w,
@@ -408,7 +433,6 @@
     over_x = Exchange("dx", send2, land2, sems.at[1])
     back_x = Exchange("dx", send3, land3, sems.at[2])
     back_y = Exchange("dy", send4, land4, sems.at[3])
-    over_y.start()
     halo = {}
     for i, b in enumerate(GHOST_BLOCKS):
         target = {
@@ -426,6 +450,7 @@
             )
             copy.start()
             halo[b, j] = copy
+    over_y.start()
 
     over_y.wait_recv()
     loads[2].wait()
@@ -451,21 +476,21 @@
 
     def edges(start, stop):
         fixed = (own, radial_w, expand_w, w_contract, sums)
+        even = (picked_even, picked_odd), (hidden_even, hidden_odd), (gains_even, gains_odd)
+        odd = tuple(pair[::-1] for pair in even)
 
         def pair(h, carry):
-            block = 2 * h
-            gather_edges(block + 1, lists, table, picked_odd, SLOTS)
-            edge_block(block, table, picked_even, *fixed)
-            following = jnp.minimum(block + 2, BLOCKS - 1)
-            gather_edges(following, lists, table, picked_even, SLOTS)
-            edge_block(block + 1, table, picked_odd, *fixed)
+            edge_step(2 * h, lists, table, *even, *fixed)
+            edge_step(2 * h + 1, lists, table, *odd, *fixed)
             return carry
 
         lax.fori_loop(start // 2, stop // 2, pair, 0)
 
     for i in (3, 7):
         loads[i].wait()
-    gather_edges(0, lists, table, picked_even, 1)
+    gather_edges(0, 0, SLOTS, lists, table, picked_even, 2)
+    gather_edges(1, 0, SLOTS, lists, table, picked_odd, 2)
+    edge_inputs(0, 0, SLOTS, table, picked_even, own, radial_w, hidden_even, gains_even)
     edges(*SHARES[0])
 
     over_x.wait_recv()
@@ -571,6 +596,10 @@
             pltpu.VMEM((EXT, 8, 128), F32),
             pltpu.VMEM((EDGES, 8, 128), F32),
             pltpu.VMEM((EDGES, 8, 128), F32),
+            pltpu.VMEM((EDGES, 128), BF),
+            pltpu.VMEM((EDGES, 128), BF),
+            pltpu.VMEM((4, SLOTS, GROUP, 128), F32),
+            pltpu.VMEM((4, SLOTS, GROUP, 128), F32),
             pltpu.VMEM((ATOMS, 128), F32),
             pltpu.VMEM((128, 128), BF),
             pltpu.VMEM((128, 1024), BF),

time: 69.7 us -> 68.5 us (0.983)
  the two profiles are of different devices: /device:TPU:1 before, /device:TPU:8 now
where the time goes in v2:
time: 68.5 us; the launch traced here: 68.3 us
  Pallas kernels  65 us (95%)
  local copies, waits for them, and re-layouts  2.71 us (4%)
    pallas_call x1, Pallas kernels, shards(): pl.pallas_call(device_kernel, out_shape=jax.ShapeDtypeStruct((3, ATOMS),...  65 us
    reshape x1, local copies, waits for them, and re-layouts, shards(): neighbour_list[0, 0].T.reshape(-1)  1.42 us

profile of v2, /device:TPU:8, one launch (start us, length us, event | category | flops | bytes accessed | tf_op | source)
XLA Modules:
  0.0 68.3 jit_solution(15772955373719725700)
XLA Ops:
  0.7 1.4 %reshape.3.lists_far = s32[12288]{0:T(1024)} reshape(s32[32,384]{1,0:T(8,128)} %bitcast.10) | data formatting | bytes 98304 | tf_op jit(solution)/shard_map/reshape | solution.py:643
  2.1 65.0 %forces.1 = f32[3,384]{1,0:T(4,128)} custom-call(s32[1,1]{1,0:T(1,128)S(6)} %copy.20.count, bf16[384,128]{1,0:T(8,128)(2,1)} %bitcast.9, bf16[3,384]{1,0:T(4,128)(2,1)} %bitcast.12, s32[1,256]{1,0:T(1,128)} %bitcast.14, s32[1,384]{1,0:T(1,128)} %bitcast.13, bf16[128,128]{1,0:T(8,128)(2,1)} %w_self.1, bf16[128,256]{1,0:T(8,128)(2,1)} %w_pair.1, ...), custom_call_target="tpu_custom_call" | custom-call | tf_op jit(solution)/shard_map/forces/pallas_call | solution.py:582
  67.0 1.3 %copy.19 = f32[1,1,3,384]{3,1,2,0:T(1,128)} copy(f32[1,1,3,384]{3,2,1,0:T(4,128)} %bitcast.11) | data formatting | bytes 9216 | tf_op jit(solution)/shard_map/broadcast_in_dim | solution.py:650
